TPU v7x, 1024 devices: a whole 4x4x32 slice. The times are simulated.
1024 devices in a mesh: dp: 64 (over z_lo, y), expert: 16 (over x, z_hi, core).
Axes of the slice: x: 4, y: 4, z: 32 (z_hi: 2, z_lo: 16; z = z_hi * 16 + z_lo), core: 2. Of those that a mesh axis runs over, the one named last changes fastest.
Arguments:
- tokens: bfloat16 [131072, 1024], P(('dp', 'expert')), may hold values from -6 to 6
- norm_gain: float32 [1024], replicated, may hold values from 0.25 to 1.75
- router_w: bfloat16 [1024, 16], replicated, may hold values from -0.1875 to 0.1875
- w_gate: bfloat16 [16, 1024, 384], P('expert'), may hold values from -0.1875 to 0.1875
- w_up: bfloat16 [16, 1024, 384], P('expert'), may hold values from -0.1875 to 0.1875
- w_down: bfloat16 [16, 384, 1024], P('expert'), may hold values from -0.3125 to 0.3125
- routes: int32 [131072, 2], P(('dp', 'expert')), may hold values from 0 to 15, all different within a row; in each aligned block of 128 rows (0 to 127, 128 to 255, ...) at most 24 rows name the same one
- grad_out: bfloat16 [131072, 1024], P(('dp', 'expert')), may hold values from -24 to 24
Outputs:
- layer_out: bfloat16 [131072, 1024], P(('dp', 'expert'))
- d_tokens: bfloat16 [131072, 1024], P(('dp', 'expert'))
- d_gain: float32 [1024], replicated
- d_router: float32 [1024, 16], replicated
- d_gate_w: float32 [16, 1024, 384], P('expert', 'dp')
- d_up_w: float32 [16, 1024, 384], P('expert', 'dp')
- d_down_w: float32 [16, 384, 1024], P('expert', None, 'dp')
Inputs may be any that keep to these rules, and one draw needn't show every extreme that they name: `routes`: each row names 2 different experts. In each aligned block of 128 rows (the rows of one device) no expert is named by more than 24 rows, a bound that some block reaches.
All inputs are finite; a program needn't handle non-finite values.
Results may differ from a plain program's by a relative error of at most 0.0073.
Values may be sent and summed in bfloat16 or wider, within the bound.
A program may use at most 64 MiB of HBM per device.

v0:
```python
import jax
import jax.numpy as jnp
from jax import lax
from jax.sharding import PartitionSpec as P

TOP = 2


contract_rows = (((0,), (0,)), ((), ()))
contract_cols = (((1,), (1,)), ((), ()))


def to_experts(buffer_rows):
    return lax.all_to_all(buffer_rows, "expert", split_axis=0, concat_axis=0, tiled=True)


def to_tokens(buffer_rows):
    return lax.all_to_all(buffer_rows, "expert", split_axis=0, concat_axis=0, tiled=True)


def local(tokens, norm_gain, router_w, w_gate, w_up, w_down, routes, grad_out):
    tok_dev, model_width = tokens.shape
    experts = lax.axis_size("expert")
    capacity = max(2, 3 * tok_dev * TOP // (2 * experts))
    tokens_wide = tokens.astype(jnp.float32)
    inverse = lax.rsqrt(jnp.mean(tokens_wide * tokens_wide, axis=1, keepdims=True) + 1e-06)
    unit_rows = tokens_wide * inverse
    normed = (unit_rows * norm_gain).astype(jnp.bfloat16)
    logits = jnp.dot(normed, router_w, preferred_element_type=jnp.float32)
    picked = jnp.take_along_axis(logits, routes, axis=1)
    gate_pair = jnp.stack(
        [jax.nn.sigmoid(picked[:, 0] - picked[:, 1]), jax.nn.sigmoid(picked[:, 1] - picked[:, 0])],
        axis=1,
    )
    flat_routes = routes.reshape(-1)
    onehot = (flat_routes[:, None] == jnp.arange(experts, dtype=jnp.int32)[None, :]).astype(
        jnp.int32
    )
    slot_index = jnp.sum((jnp.cumsum(onehot, axis=0) - onehot) * onehot, axis=1)
    placement = flat_routes * capacity + slot_index
    copied_rows = jnp.repeat(normed, TOP, axis=0)
    send_rows = (
        jnp.zeros((experts * capacity, model_width), jnp.bfloat16).at[placement].set(copied_rows)
    )
    arrived = to_experts(send_rows.reshape(experts, capacity, model_width)).reshape(-1, model_width)
    gate_local = w_gate[0]
    up_local = w_up[0]
    down_local = w_down[0]
    pre_gate = jnp.dot(arrived, gate_local, preferred_element_type=jnp.float32)
    pre_up = jnp.dot(arrived, up_local, preferred_element_type=jnp.float32)
    sigmoid_gate = jax.nn.sigmoid(pre_gate)
    active = pre_gate * sigmoid_gate
    hidden = (active * pre_up).astype(jnp.bfloat16)
    produced = jnp.dot(hidden, down_local, preferred_element_type=jnp.float32).astype(jnp.bfloat16)
    returned = to_tokens(produced.reshape(experts, capacity, model_width)).reshape(-1, model_width)
    picked_rows = returned[placement].reshape(tok_dev, TOP, model_width).astype(jnp.float32)
    layer_out = jnp.sum(gate_pair[:, :, None] * picked_rows, axis=1).astype(jnp.bfloat16)
    upstream = grad_out.astype(jnp.float32)
    d_pair = jnp.sum(upstream[:, None, :] * picked_rows, axis=2)
    d_rows = (
        (gate_pair[:, :, None] * upstream[:, None, :]).astype(jnp.bfloat16).reshape(-1, model_width)
    )
    d_send = jnp.zeros((experts * capacity, model_width), jnp.bfloat16).at[placement].set(d_rows)
    d_arrived = to_experts(d_send.reshape(experts, capacity, model_width)).reshape(-1, model_width)
    d_hidden = lax.dot_general(
        d_arrived, down_local, contract_cols, preferred_element_type=jnp.float32
    )
    d_pre_gate = (
        d_hidden * pre_up * sigmoid_gate * (1.0 + pre_gate * (1.0 - sigmoid_gate))
    ).astype(jnp.bfloat16)
    d_pre_up = (d_hidden * active).astype(jnp.bfloat16)
    d_back = (
        lax.dot_general(d_pre_gate, gate_local, contract_cols, preferred_element_type=jnp.float32)
        + lax.dot_general(d_pre_up, up_local, contract_cols, preferred_element_type=jnp.float32)
    ).astype(jnp.bfloat16)
    d_returned = to_tokens(d_back.reshape(experts, capacity, model_width)).reshape(-1, model_width)
    d_normed = jnp.sum(
        d_returned[placement].reshape(tok_dev, TOP, model_width).astype(jnp.float32), axis=1
    )
    hidden_units = gate_local.shape[1]
    d_pre_both = jnp.concatenate([d_pre_gate, d_pre_up], axis=1)
    joined = lax.psum_scatter(
        jnp.concatenate(
            [
                lax.dot_general(
                    arrived, d_pre_both, contract_rows, preferred_element_type=jnp.float32
                ),
                lax.dot_general(
                    d_arrived, hidden, contract_rows, preferred_element_type=jnp.float32
                ),
            ],
            axis=1,
        ),
        "dp",
        scatter_dimension=0,
        tiled=True,
    )
    gate_share = joined[:, :hidden_units]
    up_share = joined[:, hidden_units : 2 * hidden_units]
    down_share = joined[:, 2 * hidden_units :]
    d_first = gate_pair[:, 0] * gate_pair[:, 1] * (d_pair[:, 0] - d_pair[:, 1])
    expert_ids = jnp.arange(experts, dtype=jnp.int32)[None, :]
    d_logits = (
        (routes[:, 0:1] == expert_ids).astype(jnp.float32)
        - (routes[:, 1:2] == expert_ids).astype(jnp.float32)
    ) * d_first[:, None]
    router_wide = router_w.astype(jnp.float32)
    d_normed = d_normed + lax.dot_general(
        d_logits, router_wide, contract_cols, precision=lax.Precision.HIGHEST
    )
    router_term = lax.dot_general(
        normed.astype(jnp.float32), d_logits, contract_rows, precision=lax.Precision.HIGHEST
    )
    gain_term = jnp.sum(d_normed * unit_rows, axis=0)
    d_gain, d_router = lax.psum((gain_term, router_term), ("dp", "expert"))
    scaled_grad = d_normed * norm_gain
    d_tokens = (
        inverse
        * (scaled_grad - unit_rows * jnp.mean(scaled_grad * unit_rows, axis=1, keepdims=True))
    ).astype(jnp.bfloat16)
    return (
        layer_out,
        d_tokens,
        d_gain,
        d_router,
        gate_share[None],
        up_share[None],
        jnp.transpose(down_share)[None],
    )


def solution(mesh):
    in_specs = (
        P(("dp", "expert"), None),
        P(),
        P(),
        P("expert", None, None),
        P("expert", None, None),
        P("expert", None, None),
        P(("dp", "expert"), None),
        P(("dp", "expert"), None),
    )
    out_specs = (
        P(("dp", "expert"), None),
        P(("dp", "expert"), None),
        P(),
        P(),
        P("expert", "dp", None),
        P("expert", "dp", None),
        P("expert", None, "dp"),
    )
    return jax.shard_map(local, mesh=mesh, in_specs=in_specs, out_specs=out_specs, check_vma=False)
```

profile of v0, /device:TPU:25, one launch (start us, length us, event | category | flops | bytes accessed | tf_op | source)
XLA Modules:
  0.0 1387.5 jit_solution(12924871140193026019)
XLA Ops:
  8.0 0.8 broadcast_multiply_fusion
  8.8 0.8 copy.86
  9.6 0.1 eq.59
  9.7 0.1 eq.55
  9.8 1.1 fusion.25
  11.0 0.1 mul.147
  11.2 0.6 reduce-window.6
  11.8 0.2 slice_reduce_fusion
  12.0 1.1 fusion.19
  13.1 0.3 broadcast_in_dim.13
  13.4 0.2 reshape.169
  13.7 2.6 scatter_custom_fusion
  16.3 31.5 %all-to-all-start = ((bf16[16,24,1024]{2,1,0:T(8,128)(2,1)}), bf16[16,24,1024]{2,1,0:T(8,128)(2,1)S(1)}, u32[]{:S(2)}, u32[]{:S(2)}) async-start(bf16[16,24,1024]{2,1,0:T(8,128)(2,1)} %bitcast.4), calls=%async_computation | async-start | bytes 1572864 | tf_op jit(solution)/shard_map/all_to_all | solution.py:14
  47.8 0.1 copy.82
  47.9 0.1 reshape.159
  48.1 0.2 fusion.45
  48.3 2.0 gather_fusion.2
  50.3 0.1 reshape.162
  50.5 0.1 copy.84
  50.6 0.1 mul.152
  50.8 0.3 mul.154
  51.1 1.7 mul.155
  52.8 3.4 scatter_custom_fusion.1
  56.2 24.1 %all-to-all-done = bf16[16,24,1024]{2,1,0:T(8,128)(2,1)S(1)} async-done(((bf16[16,24,1024]{2,1,0:T(8,128)(2,1)}), bf16[16,24,1024]{2,1,0:T(8,128)(2,1)S(1)}, u32[]{:S(2)}, u32[]{:S(2)}) %all-to-all-start) | async-done | bytes 786464 | tf_op jit(solution)/shard_map/all_to_all | solution.py:14
  80.4 4.9 all-to-all-start.2
  85.3 1.4 fusion.4
  86.7 1.5 fusion.8
  88.2 49.1 %all-to-all-done.2 = bf16[16,24,1024]{2,1,0:T(8,128)(2,1)} async-done(((bf16[16,24,1024]{2,1,0:T(8,128)(2,1)}), bf16[16,24,1024]{2,1,0:T(8,128)(2,1)}, u32[]{:S(2)}, u32[]{:S(2)}) %all-to-all-start.2) | async-done | bytes 786464 | tf_op jit(solution)/shard_map/all_to_all | solution.py:14
  137.3 3.0 multiply_convert_fusion.1
  140.3 0.7 copy-done.9
  141.0 1.5 convolution_convert_fusion
  142.5 22.3 %all-to-all-start.1 = ((bf16[16,24,1024]{2,1,0:T(8,128)(2,1)}), bf16[16,24,1024]{2,1,0:T(8,128)(2,1)S(1)}, u32[]{:S(2)}, u32[]{:S(2)}) async-start(bf16[16,24,1024]{2,1,0:T(8,128)(2,1)} %bitcast.9), calls=%async_computation.1 | async-start | bytes 1572864 | tf_op jit(solution)/shard_map/all_to_all | solution.py:18
  164.8 0.2 reduce-scatter.4.cloned.1.call-start
  165.0 1.8 fusion.46
  166.9 1.0 fusion.14
  167.9 2.5 pad_maximum_fusion
  170.4 6.1 copy.95
  176.6 1.1 copy-done.4
  177.7 1.6 fusion.6
  179.3 1.5 add_convert_fusion
  180.9 43.2 %all-to-all-done.1 = bf16[16,24,1024]{2,1,0:T(8,128)(2,1)S(1)} async-done(((bf16[16,24,1024]{2,1,0:T(8,128)(2,1)}), bf16[16,24,1024]{2,1,0:T(8,128)(2,1)S(1)}, u32[]{:S(2)}, u32[]{:S(2)}) %all-to-all-start.1) | async-done | bytes 786464 | tf_op jit(solution)/shard_map/all_to_all | solution.py:18
  224.1 3.8 all-to-all-start.3
  228.0 0.9 convert_element_type.74
  228.9 2.0 gather_fusion
  230.9 1.8 reshape.141
  232.6 2.6 multiply_reduce_fusion
  235.4 107.6 %all-to-all-done.3 = bf16[16,24,1024]{2,1,0:T(8,128)(2,1)S(1)} async-done(((bf16[16,24,1024]{2,1,0:T(8,128)(2,1)}), bf16[16,24,1024]{2,1,0:T(8,128)(2,1)S(1)}, u32[]{:S(2)}, u32[]{:S(2)}) %all-to-all-start.3) | async-done | bytes 786464 | tf_op jit(solution)/shard_map/all_to_all | solution.py:18
  343.0 1.2 gather_fusion.1
  344.2 0.7 reshape.142
  344.9 1.2 reduce_sum.69
  346.2 0.6 fusion.24
  346.8 181.2 %psum.14 = f32[1024]{0:T(1024)} all-reduce(f32[1024]{0:T(1024)S(1)} %get-tuple-element.58), channel_id=1, replica_groups=mesh['dp'=64,'expert'=16] {'dp','expert'}, use_global_device_ids=true, to_apply=%region_11.12 | all-reduce | flops 1024 | bytes 8192 | tf_op jit(solution)/shard_map/psum | solution.py:115
  528.0 1.0 fusion.31
  529.0 0.9 fusion.23
  529.9 456.8 %reduce-scatter.4.cloned.1.call-done = f32[16,1152]{1,0:T(8,128)} async-done(((f32[1024,1152]{1,0:T(8,128)}), f32[16,1152]{1,0:T(8,128)}) %reduce-scatter.4.cloned.1.call-update) | async-done | bytes 73744
  986.7 0.8 fusion.43
  987.4 0.1 copy.101
  987.6 0.7 copy.94
  988.3 0.1 copy.100
  988.4 0.7 copy.93
  989.1 0.1 copy.99
  989.3 0.7 copy.92
  990.0 388.6 %all-reduce.2.cloned.1.call-done = f32[1024,16]{0,1:T(8,128)} async-done(((f32[1024,16]{0,1:T(8,128)}), f32[1024,16]{0,1:T(8,128)}) %all-reduce.2.cloned.1.call-update) | async-done | bytes 65552 | tf_op jit(solution)/shard_map/psum | solution.py:115
  1378.5 1.5 copy.105
  (50 shorter events, 0.8 us)
Async XLA Ops:
  8.0 129.3 %copy-start = (bf16[1,384,1024]{2,1,0:T(8,128)(2,1)S(1)}, bf16[1,384,1024]{2,1,0:T(8,128)(2,1)}, u32[]{:S(2)}) copy-start(bf16[1,384,1024]{2,1,0:T(8,128)(2,1)} %param.13) | copy-start | bytes 2359300
  13.4 34.4 %copy-start.14 = (s32[128,2]{0,1:T(2,128)S(1)}, s32[128,2]{0,1:T(2,128)}, u32[]{:S(2)}) copy-start(s32[128,2]{0,1:T(2,128)} %param.14) | copy-start | bytes 3076
  13.4 34.7 %copy-start.12 = (bf16[1024,16]{0,1:T(8,128)(2,1)S(1)}, bf16[1024,16]{0,1:T(8,128)(2,1)}, u32[]{:S(2)}) copy-start(bf16[1024,16]{0,1:T(8,128)(2,1)} %param.10) | copy-start | bytes 98308
  16.3 64.0 %all-to-all-start = ((bf16[16,24,1024]{2,1,0:T(8,128)(2,1)}), bf16[16,24,1024]{2,1,0:T(8,128)(2,1)S(1)}, u32[]{:S(2)}, u32[]{:S(2)}) async-start(bf16[16,24,1024]{2,1,0:T(8,128)(2,1)} %bitcast.4), calls=%async_computation | async-start | bytes 1572864 | tf_op jit(solution)/shard_map/all_to_all | solution.py:14
  48.3 2.5 copy-start.10
  52.8 32.5 %copy-start.2 = (bf16[1,1024,384]{2,1,0:T(8,128)(2,1)S(1)}, bf16[1,1024,384]{2,1,0:T(8,128)(2,1)}, u32[]{:S(2)}) copy-start(bf16[1,1024,384]{2,1,0:T(8,128)(2,1)} %param.12) | copy-start | bytes 2359300
  80.4 6.3 copy-start.3
  80.4 56.9 %all-to-all-start.2 = ((bf16[16,24,1024]{2,1,0:T(8,128)(2,1)}), bf16[16,24,1024]{2,1,0:T(8,128)(2,1)}, u32[]{:S(2)}, u32[]{:S(2)}) async-start(bf16[16,24,1024]{2,1,0:T(8,128)(2,1)} %bitcast.11), calls=%async_computation.2 | async-start | bytes 1572864 | tf_op jit(solution)/shard_map/all_to_all | solution.py:14
  140.3 0.7 copy-start.9
  142.5 81.6 %all-to-all-start.1 = ((bf16[16,24,1024]{2,1,0:T(8,128)(2,1)}), bf16[16,24,1024]{2,1,0:T(8,128)(2,1)S(1)}, u32[]{:S(2)}, u32[]{:S(2)}) async-start(bf16[16,24,1024]{2,1,0:T(8,128)(2,1)} %bitcast.9), calls=%async_computation.1 | async-start | bytes 1572864 | tf_op jit(solution)/shard_map/all_to_all | solution.py:18
  164.8 821.9 %reduce-scatter.4.cloned.1.call-start = ((), (), s32[]{:S(2)}) async-start(), calls=%async_computation.6 | async-start | bytes 4792320
  165.0 1.9 copy-start.6
  165.0 1.9 copy-start.8
  176.6 1.1 copy-start.4
  177.7 1.6 copy-start.7
  180.9 47.1 %copy-start.11 = (bf16[128,1024]{1,0:T(8,128)(2,1)S(1)}, bf16[128,1024]{1,0:T(8,128)(2,1)}, u32[]{:S(2)}) copy-start(bf16[128,1024]{1,0:T(8,128)(2,1)} %param.15) | copy-start | bytes 786436
  224.1 118.9 %all-to-all-start.3 = ((bf16[16,24,1024]{2,1,0:T(8,128)(2,1)}), bf16[16,24,1024]{2,1,0:T(8,128)(2,1)S(1)}, u32[]{:S(2)}, u32[]{:S(2)}) async-start(bf16[16,24,1024]{2,1,0:T(8,128)(2,1)} %bitcast.82), calls=%async_computation.3 | async-start | bytes 1572864 | tf_op jit(solution)/shard_map/all_to_all | solution.py:18
  227.9 1150.6 %all-reduce.2.cloned.1.call-start = ((), (), s32[]{:S(2)}) async-start(), calls=%async_computation.5 | async-start | bytes 131072 | tf_op jit(solution)/shard_map/psum | solution.py:115
  230.9 1.8 copy-start.5
  344.2 1.9 copy-start.1
  344.2 1.9 copy-start.13
Sparse Core Ops, SparseCore 0:
  176.7 809.8 reduce-scatter.3
Sparse Core Ops, SparseCore 1:
  529.1 849.4 all-reduce.1
where the time goes:
time: 1390 us
  waiting for transfers between devices  1070 us (77%)
  blocking collectives  181 us (13%)
  starting transfers between devices  62.8 us (5%)
  local copies, waits for them, and re-layouts  27.8 us (2%)
  between operations  15.8 us (1%)
  other arithmetic  15.3 us (1%)
  matrix products  15.1 us (1%)
    unnamed x3, waiting for transfers between devices  457 us
    psum x1, waiting for transfers between devices, local(): d_gain, d_router = lax.psum((gain_term, router_term), ('dp', 'expert'))  389 us
    psum x1, blocking collectives, local(): d_gain, d_router = lax.psum((gain_term, router_term), ('dp', 'expert'))  181 us
    all_to_all x2, waiting for transfers between devices, to_tokens(): lax.all_to_all(buffer_rows, 'expert', split_axis=0, concat_axis=0, tiled=...  151 us
    all_to_all x2, waiting for transfers between devices, to_experts(): lax.all_to_all(buffer_rows, 'expert', split_axis=0, concat_axis=0, tiled=...  73.2 us
    all_to_all x2, starting transfers between devices, to_experts(): lax.all_to_all(buffer_rows, 'expert', split_axis=0, concat_axis=0, tiled=...  36.4 us
  transfers between devices with their start and end apart: 6, of which 6 were waited for; matrix products, arithmetic and copies ran while one was open for 3% of the time, Pallas kernels for 0%

commit v1 on v0

v1 whole, which is shorter than its diff:
```python
import jax
import jax.numpy as jnp
from jax import lax
from jax.experimental import pallas as pl
from jax.experimental.pallas import tpu as pltpu
from jax.sharding import PartitionSpec as P

TOP = 2
MESH = pl.DeviceIdType.MESH
ANY = pl.BlockSpec(memory_space=pl.ANY)
VMEM = pl.BlockSpec(memory_space=pltpu.VMEM)
LIMIT = 48 * 1024 * 1024

contract_rows = (((0,), (0,)), ((), ()))
contract_cols = (((1,), (1,)), ((), ()))


class Place:
    def __init__(self):
        dp, ex = lax.axis_index("dp"), lax.axis_index("expert")
        self.y, self.zl = lax.rem(dp, 4), lax.div(dp, 4)
        self.a, self.b = lax.div(self.zl, 4), lax.rem(self.zl, 4)
        self.x, self.zh, self.core = lax.div(ex, 4), lax.rem(lax.div(ex, 2), 2), lax.rem(ex, 2)
        self.yhi = lax.div(self.y, 2)
        self.ylow = self.y + self.yhi * (3 - 2 * self.y)
        zexp = self.zh + self.yhi - 2 * self.zh * self.yhi
        self.me = self.x * 4 + zexp * 2 + self.core

    def at(self, x=None, y=None, zl=None, zh=None, core=None):
        x = self.x if x is None else x
        y = self.y if y is None else y
        zl = self.zl if zl is None else zl
        zh = self.zh if zh is None else zh
        core = self.core if core is None else core
        return (zl * 4 + y, x * 4 + zh * 2 + core)

    def member(self, h):
        x, zexp, core = lax.div(h, 4), lax.rem(lax.div(h, 2), 2), lax.rem(h, 2)
        hi = zexp + self.zh - 2 * zexp * self.zh
        return self.at(x=x, y=self.ylow + hi * (3 - 2 * self.ylow), core=core)

    def zglobal(self, step):
        z = lax.rem(self.zh * 16 + self.zl + 32 + step, 32)
        return self.at(zl=lax.rem(z, 16), zh=lax.div(z, 16))


def signal(device):
    pl.semaphore_signal(pltpu.get_barrier_semaphore(), inc=1, device_id=device, device_id_type=MESH)


def remote(src, dst, send_sem, recv_sem, device):
    return pltpu.make_async_remote_copy(
        src_ref=src, dst_ref=dst, send_sem=send_sem, recv_sem=recv_sem, device_id=device, device_id_type=MESH
    )


def exchange(place, send, recv, send_sem, recv_sem, own_sem):
    own = pltpu.make_async_copy(send.at[place.me], recv.at[place.me], own_sem)
    own.start()
    copies = []
    for k in range(1, 16):
        h = lax.rem(place.me + k, 16)
        copy = remote(send.at[h], recv.at[place.me], send_sem.at[k], recv_sem.at[k], place.member(h))
        copy.start()
        copies.append(copy)
    return own, copies


def dispatch_kernel(
    send, gate, up, down, recv, gate_out, up_out, down_out,
    send_sem, recv_sem, own_sem, first_sem, fwd_sem, side_sem, from_z, from_y, keep_sem,
):
    p = Place()
    for k in range(1, 16):
        signal(p.member(lax.rem(p.me + k, 16)))
    foreign = p.yhi == 1
    after = jnp.where(p.zl == 7, 0, 1)
    before = jnp.where(p.zl == 8, 0, 1)
    sibling = p.at(y=p.y + 1 - 2 * lax.rem(p.y, 2))

    @pl.when(foreign)
    def _():
        signal(sibling)

    @pl.when(jnp.logical_and(foreign, p.zl != 7))
    def _():
        signal(p.zglobal(1))

    @pl.when(jnp.logical_and(foreign, p.zl != 8))
    def _():
        signal(p.zglobal(-1))

    pl.semaphore_wait(pltpu.get_barrier_semaphore(), 15 + p.yhi * (1 + after + before))

    pairs = ((gate, gate_out), (up, up_out), (down, down_out))
    rows = [src.shape[0] // 8 for src, _ in pairs]
    half = lax.rem(p.y, 2)

    def piece(n, ref, side, c):
        return ref.at[pl.ds(pl.multiple_of((side * 4 + c) * rows[n], 16), rows[n])]

    def boundary(n, c, to):
        src, dst = pairs[n]
        return remote(
            piece(n, src, half, c), piece(n, dst, half, c), first_sem.at[n * 4 + c], from_z.at[n * 4 + c], to
        )

    def onward(n, c, to):
        dst = pairs[n][1]
        return remote(piece(n, dst, half, c), piece(n, dst, half, c), fwd_sem.at[n * 4 + c], from_z.at[n * 4 + c], to)

    def sideways(n, c):
        dst = pairs[n][1]
        return remote(
            piece(n, dst, half, c), piece(n, dst, half, c), side_sem.at[n * 4 + c], from_y.at[n * 4 + c], sibling
        )

    def each(body):
        for n in range(3):
            def step(c, carry, n=n):
                body(n, c)
                return carry
            lax.fori_loop(0, 4, step, 0)

    edge = jnp.logical_or(p.zl == 0, p.zl == 15)
    outward = p.zglobal(jnp.where(p.zl == 0, -1, 1))
    inward = p.at(zl=p.zl + jnp.where(p.zl < 8, 1, -1))
    passes = jnp.logical_and(p.zl != 7, p.zl != 8)

    @pl.when(jnp.logical_and(foreign, edge))
    def _():
        each(lambda n, c: boundary(n, c, outward).start())

    own, copies = exchange(p, send, recv, send_sem, recv_sem, own_sem)

    @pl.when(jnp.logical_not(foreign))
    def _():
        kept = [pltpu.make_async_copy(src, dst, keep_sem.at[n]) for n, (src, dst) in enumerate(pairs)]
        for copy in kept:
            copy.start()
        for copy in kept:
            copy.wait()

    @pl.when(foreign)
    def _():
        def take(n, c):
            onward(n, c, inward).wait_recv()

            @pl.when(passes)
            def _():
                onward(n, c, inward).start()

            sideways(n, c).start()

        each(take)
        each(lambda n, c: sideways(n, c).wait())

    @pl.when(jnp.logical_and(foreign, passes))
    def _():
        each(lambda n, c: onward(n, c, inward).wait_send())

    @pl.when(jnp.logical_and(foreign, edge))
    def _():
        each(lambda n, c: boundary(n, c, outward).wait_send())

    own.wait()
    for copy in copies:
        copy.wait()


def dispatch(send, gate, up, down):
    dma = pltpu.SemaphoreType.DMA
    return pl.pallas_call(
        dispatch_kernel,
        out_shape=[jax.ShapeDtypeStruct(v.shape, v.dtype) for v in (send, gate, up, down)],
        in_specs=[ANY] * 4,
        out_specs=[ANY] * 4,
        scratch_shapes=[
            dma((16,)), dma((16,)), dma(()), dma((12,)), dma((12,)), dma((12,)), dma((12,)), dma((12,)), dma((3,)),
        ],
        compiler_params=pltpu.CompilerParams(collective_id=0, has_side_effects=True, vmem_limit_bytes=LIMIT),
    )(send, gate, up, down)


def return_kernel(
    send, part, recv, total,
    y_got, held, z_got, send_sem, recv_sem, own_sem, y_send, y_recv, z_send, z_recv,
):
    p = Place()
    sibling = p.at(y=p.y + 1 - 2 * lax.rem(p.y, 2))
    for k in range(1, 16):
        signal(p.member(lax.rem(p.me + k, 16)))
    signal(sibling)
    for k in range(1, 4):
        signal(p.at(zl=p.a * 4 + lax.rem(p.b + k, 4)))
    pl.semaphore_wait(pltpu.get_barrier_semaphore(), 19)

    side = p.ylow
    y_copies = []
    for k in range(4):
        bb = lax.rem(p.b + k + 1, 4)
        copy = remote(part.at[1 - side, bb], y_got.at[bb], y_send.at[k], y_recv.at[k], sibling)
        copy.start()
        y_copies.append(copy)
    own, copies = exchange(p, send, recv, send_sem, recv_sem, own_sem)
    z_copies = []
    for k in range(4):
        bb = lax.rem(p.b + k + 1, 4)
        y_copies[k].wait_recv()
        both = part[side, bb].astype(jnp.float32) + y_got[bb].astype(jnp.float32)
        if k == 3:
            for copy in z_copies:
                copy.wait_recv()
            for j in range(3):
                both = both + z_got[j].astype(jnp.float32)
            total[...] = both.astype(jnp.bfloat16)
        else:
            held[k] = both.astype(jnp.bfloat16)
            copy = remote(held.at[k], z_got.at[k], z_send.at[k], z_recv.at[k], p.at(zl=p.a * 4 + bb))
            copy.start()
            z_copies.append(copy)
    for copy in y_copies + z_copies:
        copy.wait_send()
    own.wait()
    for copy in copies:
        copy.wait()


def give_back(send, part):
    dma = pltpu.SemaphoreType.DMA
    block = part.shape[2:]
    return pl.pallas_call(
        return_kernel,
        out_shape=[jax.ShapeDtypeStruct(send.shape, send.dtype), jax.ShapeDtypeStruct(block, jnp.bfloat16)],
        in_specs=[ANY, VMEM],
        out_specs=[ANY, VMEM],
        scratch_shapes=[
            pltpu.VMEM((4,) + block, jnp.bfloat16),
            pltpu.VMEM((3,) + block, jnp.bfloat16),
            pltpu.VMEM((3,) + block, jnp.bfloat16),
            dma((16,)), dma((16,)), dma(()), dma((4,)), dma((4,)), dma((3,)), dma((3,)),
        ],
        compiler_params=pltpu.CompilerParams(collective_id=1, has_side_effects=True, vmem_limit_bytes=LIMIT),
    )(send, part)


def finish_kernel(
    part, small, share, small_out,
    z_got, leaving, native, other, g1, mine, g2, g3, g4, whole,
    z_send, z_recv, f_send, f_recv, s1, r1, s2, r2, s3, r3, s4, r4, s5, r5,
):
    p = Place()
    xc = p.x * 2 + p.core

    def xc_at(t):
        return p.at(x=lax.div(t, 2), core=lax.rem(t, 2))

    def y_at(t):
        return p.at(y=t)

    def b_at(t):
        return p.at(zl=p.a * 4 + t)

    def c_at(t):
        return p.at(zl=lax.rem(t, 4) * 4 + p.b, zh=lax.div(t, 4))

    ci = p.zh * 4 + p.a
    for k in range(1, 8):
        signal(xc_at(lax.rem(xc + k, 8)))
        signal(c_at(lax.rem(ci + k, 8)))
    for k in range(1, 4):
        signal(y_at(lax.rem(p.y + k, 4)))
        signal(b_at(lax.rem(p.b + k, 4)))
    signal(p.at(y=3 - p.y, zh=1 - p.zh))
    pl.semaphore_wait(pltpu.get_barrier_semaphore(), 21)

    z_copies = []
    for k in range(3):
        aa = lax.rem(p.a + k + 1, 4)
        copy = remote(part.at[aa], z_got.at[k], z_send.at[k], z_recv.at[k], p.at(zl=aa * 4 + p.b))
        copy.start()
        z_copies.append(copy)

    def lanes(t):
        return pl.ds(pl.multiple_of(t * 128, 128), 128)

    first = []
    for k in range(1, 8):
        t = lax.rem(xc + k, 8)
        copy = remote(small.at[:, lanes(t)], g1.at[k], s1.at[k], r1.at[k], xc_at(t))
        copy.start()
        first.append(copy)

    value = small[:, lanes(xc)]
    for copy in first:
        copy.wait()
    for k in range(1, 8):
        value = value + g1[k]

    def everywhere(value, slots, n, index, where, send_sem, recv_sem, stage):
        slots[index] = value
        copies = []
        for k in range(1, n):
            copy = remote(
                slots.at[index], slots.at[index], send_sem.at[k], recv_sem.at[k], where(lax.rem(index + k, n))
            )
            copy.start()
            copies.append(copy)
        for copy in copies:
            copy.wait()
        value = slots[0]
        for k in range(1, n):
            value = value + slots[k]
        return value

    value = everywhere(value, g2, 4, p.y, y_at, s2, r2, 0)
    value = everywhere(value, g3, 4, p.b, b_at, s3, r3, 1)

    for copy in z_copies:
        copy.wait()
    summed = part[p.a].astype(jnp.float32)
    for k in range(3):
        summed = summed + z_got[k].astype(jnp.float32)
    leaving[...] = summed.astype(jnp.bfloat16).reshape(leaving.shape)
    native_rows = summed[: summed.shape[0] // 2]

    foreign = p.yhi == 1
    to_native = remote(leaving.at[1], native, f_send.at[0], f_recv.at[0], p.at(y=3 - p.y))
    cross_low = remote(leaving.at[0], other, f_send.at[0], f_recv.at[1], p.at(y=3 - p.y, zh=1 - p.zh))
    cross_high = remote(leaving.at[1], other, f_send.at[1], f_recv.at[1], p.at(zh=1 - p.zh))

    @pl.when(jnp.logical_not(foreign))
    def _():
        to_native.start()

    @pl.when(foreign)
    def _():
        cross_low.start()
        cross_high.start()

    value = everywhere(value, g4, 8, ci, c_at, s4, r4, 2)
    whole[...] = value
    small_out[:, lanes(xc)] = value
    last = []
    for k in range(1, 8):
        copy = remote(whole, small_out.at[:, lanes(xc)], s5.at[k], r5.at[k], xc_at(lax.rem(xc + k, 8)))
        copy.start()
        last.append(copy)

    cross_high.wait_recv()

    @pl.when(jnp.logical_not(foreign))
    def _():
        to_native.wait_send()
        share[...] = native_rows + other[...].astype(jnp.float32)

    @pl.when(foreign)
    def _():
        cross_low.wait_send()
        cross_high.wait_send()
        to_native.wait_recv()
        share[...] = native[...].astype(jnp.float32) + other[...].astype(jnp.float32)

    for copy in last:
        copy.wait()


def finish(part, small):
    dma = pltpu.SemaphoreType.DMA
    rows, width = part.shape[1] // 2, part.shape[2]
    tall = small.shape[0]
    f32 = jnp.float32
    return pl.pallas_call(
        finish_kernel,
        out_shape=[jax.ShapeDtypeStruct((rows, width), f32), jax.ShapeDtypeStruct(small.shape, f32)],
        in_specs=[VMEM, VMEM],
        out_specs=[VMEM, VMEM],
        scratch_shapes=[
            pltpu.VMEM((3, 2 * rows, width), jnp.bfloat16),
            pltpu.VMEM((2, rows, width), jnp.bfloat16),
            pltpu.VMEM((rows, width), jnp.bfloat16),
            pltpu.VMEM((rows, width), jnp.bfloat16),
            pltpu.VMEM((8, tall, 128), f32),
            pltpu.VMEM((tall, 128), f32),
            pltpu.VMEM((4, tall, 128), f32),
            pltpu.VMEM((4, tall, 128), f32),
            pltpu.VMEM((8, tall, 128), f32),
            pltpu.VMEM((tall, 128), f32),
            dma((3,)), dma((3,)), dma((2,)), dma((2,)),
            dma((8,)), dma((8,)), dma((4,)), dma((4,)), dma((4,)), dma((4,)),
            dma((8,)), dma((8,)), dma((8,)), dma((8,)),
        ],
        compiler_params=pltpu.CompilerParams(collective_id=2, has_side_effects=True, vmem_limit_bytes=LIMIT),
    )(part, small)


def local(tokens, norm_gain, router_w, w_gate, w_up, w_down, routes, grad_out):
    f32, bf16 = jnp.float32, jnp.bfloat16
    tok_dev, width = tokens.shape
    experts = lax.axis_size("expert")
    capacity = max(2, 3 * tok_dev * TOP // (2 * experts))
    tokens_wide = tokens.astype(f32)
    inverse = lax.rsqrt(jnp.mean(tokens_wide * tokens_wide, axis=1, keepdims=True) + 1e-06)
    unit_rows = tokens_wide * inverse
    normed = (unit_rows * norm_gain).astype(bf16)
    logits = jnp.dot(normed, router_w, preferred_element_type=f32)
    expert_ids = jnp.arange(experts, dtype=jnp.int32)[None, :]
    chosen = [routes[:, k : k + 1] == expert_ids for k in range(TOP)]
    picked = [jnp.sum(jnp.where(hot, logits, 0.0), axis=1) for hot in chosen]
    gate_pair = [jax.nn.sigmoid(picked[0] - picked[1]), jax.nn.sigmoid(picked[1] - picked[0])]

    token_ids = jnp.arange(tok_dev, dtype=jnp.int32)
    earlier = (token_ids[:, None] > token_ids[None, :]).astype(bf16)
    named = jnp.logical_or(chosen[0], chosen[1]).astype(bf16)
    ahead = jnp.dot(earlier, named, preferred_element_type=f32)
    slots = [
        routes[:, k] * (2 * capacity) + jnp.sum(jnp.where(chosen[k], ahead, 0.0), axis=1).astype(jnp.int32)
        for k in range(TOP)
    ]
    places = jnp.arange(experts * 2 * capacity, dtype=jnp.int32)
    hits = [places[:, None] == slot[None, :] for slot in slots]
    d_hits = [places[:, None] == slot[None, :] + capacity for slot in slots]
    pick = jnp.concatenate(
        [jnp.logical_or(hits[0], hits[1]).astype(bf16), jnp.logical_or(d_hits[0], d_hits[1]).astype(bf16)], axis=1
    )
    scale = jnp.sum(
        jnp.where(d_hits[0], gate_pair[0][None, :], 0.0) + jnp.where(d_hits[1], gate_pair[1][None, :], 0.0), axis=1
    )
    is_row = lax.rem(places, 2 * capacity) < capacity
    scale = jnp.where(is_row, 1.0, scale)
    stacked = jnp.concatenate([normed, grad_out], axis=0)
    send = (jnp.dot(pick, stacked, preferred_element_type=f32) * scale[:, None]).astype(bf16)
    arrived_both, gate_local, up_local, down_local = dispatch(
        send.reshape(experts, 2 * capacity, width), w_gate[0], w_up[0], w_down[0]
    )
    arrived = arrived_both[:, :capacity].reshape(-1, width)
    d_arrived = arrived_both[:, capacity:].reshape(-1, width)

    pre_gate = jnp.dot(arrived, gate_local, preferred_element_type=f32)
    pre_up = jnp.dot(arrived, up_local, preferred_element_type=f32)
    sigmoid_gate = jax.nn.sigmoid(pre_gate)
    active = pre_gate * sigmoid_gate
    hidden = (active * pre_up).astype(bf16)
    produced = jnp.dot(hidden, down_local, preferred_element_type=f32).astype(bf16)
    d_hidden = lax.dot_general(d_arrived, down_local, contract_cols, preferred_element_type=f32)
    d_pre_gate = (d_hidden * pre_up * sigmoid_gate * (1.0 + pre_gate * (1.0 - sigmoid_gate))).astype(bf16)
    d_pre_up = (d_hidden * active).astype(bf16)
    d_back = (
        lax.dot_general(d_pre_gate, gate_local, contract_cols, preferred_element_type=f32)
        + lax.dot_general(d_pre_up, up_local, contract_cols, preferred_element_type=f32)
    ).astype(bf16)
    hidden_units = gate_local.shape[1]
    d_pre_both = jnp.concatenate([d_pre_gate, d_pre_up], axis=1)
    joined = jnp.concatenate(
        [
            lax.dot_general(arrived, d_pre_both, contract_rows, preferred_element_type=f32).astype(bf16),
            lax.dot_general(d_arrived, hidden, contract_rows, preferred_element_type=f32).astype(bf16),
        ],
        axis=1,
    )
    rows = width // lax.axis_size("dp")
    blocks = joined.reshape(4, 4, 4, rows, 3 * hidden_units)
    halves = [jnp.stack([blocks[:, :, i], blocks[:, :, 3 - i]], axis=2) for i in range(2)]
    part = jnp.stack(halves, axis=0).transpose(0, 2, 1, 3, 4, 5).reshape(2, 4, 8 * rows, 3 * hidden_units)

    back = jnp.concatenate(
        [produced.reshape(experts, capacity, width), d_back.reshape(experts, capacity, width)], axis=1
    )
    returned, part = give_back(back, part)
    returned = returned.reshape(-1, width)
    pull = jnp.concatenate([hits[0], hits[1], jnp.logical_or(d_hits[0], d_hits[1])], axis=1).astype(bf16)
    pulled = lax.dot_general(pull, returned, contract_rows, preferred_element_type=f32)
    rows_0, rows_1, d_normed = pulled[:tok_dev], pulled[tok_dev : 2 * tok_dev], pulled[2 * tok_dev :]
    layer_out = (gate_pair[0][:, None] * rows_0 + gate_pair[1][:, None] * rows_1).astype(bf16)
    upstream = grad_out.astype(f32)
    d_pair = [jnp.sum(upstream * rows_0, axis=1), jnp.sum(upstream * rows_1, axis=1)]
    d_first = gate_pair[0] * gate_pair[1] * (d_pair[0] - d_pair[1])
    d_logits = (chosen[0].astype(f32) - chosen[1].astype(f32)) * d_first[:, None]
    router_wide = router_w.astype(f32)
    d_normed = d_normed + lax.dot_general(d_logits, router_wide, contract_cols, precision=lax.Precision.HIGHEST)
    router_term = lax.dot_general(d_logits, normed.astype(f32), contract_rows, precision=lax.Precision.HIGHEST)
    gain_term = jnp.sum(d_normed * unit_rows, axis=0, keepdims=True)
    small = jnp.concatenate([router_term, gain_term, jnp.zeros((24 - experts - 1, width), f32)], axis=0)
    share, small = finish(part.reshape(4, 2 * rows, 3 * hidden_units), small)
    scaled_grad = d_normed * norm_gain
    d_tokens = (
        inverse * (scaled_grad - unit_rows * jnp.mean(scaled_grad * unit_rows, axis=1, keepdims=True))
    ).astype(bf16)
    return (
        layer_out,
        d_tokens,
        small[experts],
        jnp.transpose(small[:experts]),
        share[None, :, :hidden_units],
        share[None, :, hidden_units : 2 * hidden_units],
        jnp.transpose(share[:, 2 * hidden_units :])[None],
    )


def solution(mesh):
    rows, experts, copied = P(("dp", "expert"), None), P("expert", None, None), P()
    return jax.shard_map(
        local,
        mesh=mesh,
        in_specs=(rows, copied, copied, experts, experts, experts, rows, rows),
        out_specs=(
            rows,
            rows,
            copied,
            copied,
            P("expert", "dp", None),
            P("expert", "dp", None),
            P("expert", None, "dp"),
        ),
        check_vma=False,
    )
```

time: 1390 us -> 215 us (0.15)
  waiting for transfers between devices: 1070 us -> 0 us
  Pallas kernels: 0 us -> 185 us
  blocking collectives: 181 us -> 0 us
  starting transfers between devices: 62.8 us -> 0 us
  local copies, waits for them, and re-layouts: 27.8 us -> 11.1 us
  between operations: 15.8 us -> 0.87 us
    unnamed x3 -> x0, waiting for transfers between devices: 457 us -> none
    psum x1 -> x0, waiting for transfers between devices: 389 us -> none  [local(): d_gain, d_router = lax.psum((gain_term, router_term), ('dp', 'expert'))]
    all_to_all x4 -> x0, waiting for transfers between devices: 224 us -> none  [the longest x2 151 us: to_tokens(): lax.all_to_all(buffer_rows, 'expert', split_axis=0, concat_axis=0, tiled=...]
    pallas_call x0 -> x3, Pallas kernels: none -> 185 us  [the longest x1 87.9 us: finish(): pl.pallas_call(finish_kernel, out_shape=[jax.ShapeDtypeStruct((rows, widt...]
    psum x1 -> x0, blocking collectives: 181 us -> none  [local(): d_gain, d_router = lax.psum((gain_term, router_term), ('dp', 'expert'))]
    all_to_all x4 -> x0, starting transfers between devices: 62.5 us -> none  [the longest x2 36.4 us: to_experts(): lax.all_to_all(buffer_rows, 'expert', split_axis=0, concat_axis=0, tiled=...]
  transfers between devices with their start and end apart: 6 -> 0, of which waited for: 6 -> 0; matrix products, arithmetic and copies ran while one was open for 3% -> 0% of each run, Pallas kernels for 0% -> 0%
where the time goes in v1:
time: 215 us
  Pallas kernels  185 us (86%)
  local copies, waits for them, and re-layouts  11.1 us (5%)
  matrix products  10.2 us (5%)
  other arithmetic  7.48 us (3%)
    pallas_call x1, Pallas kernels, finish(): pl.pallas_call(finish_kernel, out_shape=[jax.ShapeDtypeStruct((rows, widt...  87.9 us
    pallas_call x1, Pallas kernels, dispatch(): pl.pallas_call(dispatch_kernel, out_shape=[jax.ShapeDtypeStruct(v.shape,...  51.5 us
    pallas_call x1, Pallas kernels, give_back(): pl.pallas_call(return_kernel, out_shape=[jax.ShapeDtypeStruct(send.shape,...  45.9 us
    concatenate x1, local copies, waits for them, and re-layouts, local(): jnp.concatenate([lax.dot_general(arrived, d_pre_both, contract_rows, pref...  4.34 us

profile of v1, /device:TPU:25, one launch (start us, length us, event | category | flops | bytes accessed | tf_op | source)
XLA Modules:
  0.0 214.9 jit_solution(1884748443225631444)
XLA Ops:
  0.6 0.0 copy-start
  0.6 0.8 slice_bitcast_fusion.5
  1.4 0.1 fusion.30
  1.5 1.1 fusion.23
  2.7 1.1 fusion.17
  3.7 0.0 copy-done
  3.8 0.2 select_reduce_fusion.3
  4.0 0.8 broadcast_add_fusion.1
  4.7 0.2 add_reduce_fusion
  4.9 0.2 iota_compare_fusion.3
  5.2 0.0 copy-start.1
  5.2 0.0 copy-start.2
  5.2 0.0 copy-start.3
  5.2 2.8 %multiply_convert_fusion = bf16[768,1024]{1,0:T(8,128)(2,1)} fusion(f32[768]{0:T(1024)S(1)} %fusion.43, pred[768,128]{1,0:T(32,128)(4,1)S(1)} %get-tuple-element.58, pred[768,128]{1,0:T(32,128)(4,1)S(1)} %get-tuple-element.55, bf16[128,1024]{1,0:T(8,128)(2,1)} %param.15, bf16[128,1024]{1,0:T(8,128)(2,1)S(1)} %fusion.17), kind=kOutput, calls=%fused_computation | convolution fusion | flops 405471232 | bytes 2296832 | tf_op jit(solution)/shard_map/dot_general | solution.py:432
  8.1 0.0 copy-done.1
  8.1 0.0 copy-done.2
  8.1 0.0 copy-done.3
  8.1 51.5 %shard_map.135 = (bf16[16,48,1024]{2,1,0:T(8,128)(2,1)}, bf16[1024,384]{1,0:T(8,128)(2,1)S(1)}, bf16[1024,384]{1,0:T(8,128)(2,1)S(1)}, bf16[384,1024]{1,0:T(8,128)(2,1)S(1)}) custom-call(bf16[16,48,1024]{2,1,0:T(8,128)(2,1)} %bitcast.75, bf16[1024,384]{1,0:T(8,128)(2,1)S(1)} %bitcast.61, bf16[1024,384]{1,0:T(8,128)(2,1)S(1)} %bitcast.62, ...), custom_call_target="tpu_custom_call" | custom-call | tf_op jit(solution)/shard_map/pallas_call | solution.py:173
  59.6 1.5 fusion.49
  61.1 0.6 fusion.50
  61.7 0.6 fusion.51
  62.3 0.8 multiply_convert_fusion.3
  63.1 0.6 fusion.52
  63.7 0.6 add_convert_fusion
  64.3 0.6 convolution_convert_fusion.2
  64.9 0.2 pad_maximum_fusion.1.send
  65.1 0.6 convolution_convert_fusion.1
  65.7 1.0 convolution_convert_fusion
  66.7 1.6 pad_maximum_fusion
  68.3 4.3 %copy.20 = bf16[1024,1152]{1,0:T(8,128)(2,1)} copy(bf16[1024,1152]{0,1:T(8,128)(2,1)} %pad_maximum_fusion) | data formatting | bytes 4718592 | tf_op jit(solution)/shard_map/concatenate | solution.py:454
  72.6 0.0 copy-start.4
  72.6 1.5 slice_bitcast_fusion
  74.2 0.5 copy-done.4
  74.7 0.1 fusion.48
  74.8 0.1 maximum_bitcast_fusion.1
  74.9 0.2 maximum_bitcast_fusion
  75.1 0.2 copy.21
  75.4 45.9 %shard_map.136 = (bf16[16,48,1024]{2,1,0:T(8,128)(2,1)S(1)}, bf16[128,1152]{1,0:T(8,128)(2,1)S(1)}) custom-call(bf16[16,48,1024]{2,1,0:T(8,128)(2,1)S(1)} %pad_maximum_fusion.1.send, bf16[2,4,128,1152]{3,2,1,0:T(8,128)(2,1)S(1)} %bitcast.60), custom_call_target="tpu_custom_call" | custom-call | tf_op jit(solution)/shard_map/pallas_call | solution.py:232
  121.3 0.0 copy-start.6
  121.3 0.8 fusion
  122.2 0.1 copy-done.6
  122.3 0.0 copy-start.5
  122.3 0.0 copy-start.7
  122.3 0.9 fusion.25
  123.2 0.0 copy-done.5
  123.2 0.0 copy-done.7
  123.2 0.6 fusion.22
  123.8 0.9 fusion.21
  124.8 0.2 fusion.32
  125.0 0.1 pad.2.clone
  125.1 0.1 maximum_maximum_fusion.small
  125.1 87.9 %shard_map.137 = (f32[16,1152]{1,0:T(8,128)S(1)}, f32[24,1024]{1,0:T(8,128)S(1)}) custom-call(bf16[4,32,1152]{2,1,0:T(8,128)(2,1)S(1)} %bitcast.64, f32[24,1024]{1,0:T(8,128)S(1)} %maximum_maximum_fusion.small), custom_call_target="tpu_custom_call" | custom-call | tf_op jit(solution)/shard_map/pallas_call | solution.py:373
  213.1 0.6 slice.56
  213.7 0.6 slice_bitcast_fusion.1
  214.3 0.6 slice_bitcast_fusion.2
  (6 shorter events, 0.0 us)
Async XLA Ops:
  0.6 3.1 %copy-start = (bf16[1024,16]{0,1:T(8,128)(2,1)S(1)}, bf16[1024,16]{0,1:T(8,128)(2,1)}, u32[]{:S(2)}) copy-start(bf16[1024,16]{0,1:T(8,128)(2,1)} %param.10) | copy-start | bytes 98308
  5.2 2.9 %copy-start.1 = (bf16[1,1024,384]{2,1,0:T(8,128)(2,1)S(1)}, bf16[1,1024,384]{2,1,0:T(8,128)(2,1)}, u32[]{:S(2)}) copy-start(bf16[1,1024,384]{2,1,0:T(8,128)(2,1)} %param.11) | copy-start | bytes 2359300
  5.2 2.9 %copy-start.2 = (bf16[1,1024,384]{2,1,0:T(8,128)(2,1)S(1)}, bf16[1,1024,384]{2,1,0:T(8,128)(2,1)}, u32[]{:S(2)}) copy-start(bf16[1,1024,384]{2,1,0:T(8,128)(2,1)} %param.12) | copy-start | bytes 2359300
  5.2 2.9 %copy-start.3 = (bf16[1,384,1024]{2,1,0:T(8,128)(2,1)S(1)}, bf16[1,384,1024]{2,1,0:T(8,128)(2,1)}, u32[]{:S(2)}) copy-start(bf16[1,384,1024]{2,1,0:T(8,128)(2,1)} %param.13) | copy-start | bytes 2359300
  72.6 2.0 copy-start.4
  121.3 1.0 copy-start.6
  122.3 1.0 copy-start.5
  122.3 1.0 copy-start.7

commit v2 on v1

v2 whole, which is shorter than its diff:
```python
import jax
import jax.numpy as jnp
from jax import lax
from jax.experimental import pallas as pl
from jax.experimental.pallas import tpu as pltpu
from jax.sharding import PartitionSpec as P

TOP = 2
MESH = pl.DeviceIdType.MESH
ANY = pl.BlockSpec(memory_space=pl.ANY)
VMEM = pl.BlockSpec(memory_space=pltpu.VMEM)
LIMIT = 48 * 1024 * 1024

contract_rows = (((0,), (0,)), ((), ()))
contract_cols = (((1,), (1,)), ((), ()))


class Place:
    def __init__(self):
        dp, ex = lax.axis_index("dp"), lax.axis_index("expert")
        self.y, self.zl = lax.rem(dp, 4), lax.div(dp, 4)
        self.a, self.b = lax.div(self.zl, 4), lax.rem(self.zl, 4)
        self.x, self.zh, self.core = lax.div(ex, 4), lax.rem(lax.div(ex, 2), 2), lax.rem(ex, 2)
        self.far = lax.rem(lax.div(self.y + 1, 2) + 1, 2)
        self.side = lax.div(self.y, 2)
        self.zexp = self.zh + self.far - 2 * self.zh * self.far
        self.me = self.x * 4 + self.zexp * 2 + self.core

    def at(self, x=None, y=None, zl=None, zh=None, core=None):
        x = self.x if x is None else x
        y = self.y if y is None else y
        zl = self.zl if zl is None else zl
        zh = self.zh if zh is None else zh
        core = self.core if core is None else core
        return (zl * 4 + y, x * 4 + zh * 2 + core)

    def worker(self, far):
        return (1 - far) * (1 - self.side) + (2 + far) * self.side

    def member(self, h):
        x, zexp, core = lax.div(h, 4), lax.rem(lax.div(h, 2), 2), lax.rem(h, 2)
        return self.at(x=x, y=self.worker(zexp + self.zh - 2 * zexp * self.zh), core=core)

    def zglobal(self, step):
        z = lax.rem(self.zh * 16 + self.zl + 32 + step, 32)
        return self.at(zl=lax.rem(z, 16), zh=lax.div(z, 16))


def signal(device):
    pl.semaphore_signal(pltpu.get_barrier_semaphore(), inc=1, device_id=device, device_id_type=MESH)


def remote(src, dst, send_sem, recv_sem, device):
    return pltpu.make_async_remote_copy(
        src_ref=src, dst_ref=dst, send_sem=send_sem, recv_sem=recv_sem, device_id=device, device_id_type=MESH
    )


def exchange(place, send, recv, send_sem, recv_sem, own_sem):
    own = pltpu.make_async_copy(send.at[place.me], recv.at[place.me], own_sem)
    own.start()
    copies = []
    for k in range(1, 16):
        h = lax.rem(place.me + k, 16)
        copy = remote(send.at[h], recv.at[place.me], send_sem.at[k], recv_sem.at[k], place.member(h))
        copy.start()
        copies.append(copy)
    return own, copies


def dispatch_kernel(
    send, gate, up, down, recv, gate_out, up_out, down_out,
    send_sem, recv_sem, own_sem, first_sem, fwd_sem, side_sem, from_z, from_y, keep_sem,
):
    p = Place()
    for k in range(1, 16):
        signal(p.member(lax.rem(p.me + k, 16)))
    far = p.far == 1
    after = jnp.where(p.zl == 7, 0, 1)
    before = jnp.where(p.zl == 8, 0, 1)
    sibling = p.at(y=3 - p.y)

    @pl.when(far)
    def _():
        signal(sibling)

    @pl.when(jnp.logical_and(far, p.zl != 7))
    def _():
        signal(p.zglobal(1))

    @pl.when(jnp.logical_and(far, p.zl != 8))
    def _():
        signal(p.zglobal(-1))

    pl.semaphore_wait(pltpu.get_barrier_semaphore(), 15 + p.far * (1 + after + before))

    pairs = ((gate, gate_out, 8), (up, up_out, 8), (down, down_out, 6))
    first_of = (0, 8, 16)

    def piece(n, ref, c):
        half = pairs[n][0].shape[0] // 2
        step = half // pairs[n][2]
        return ref.at[pl.ds(pl.multiple_of(p.side * half + c * step, 16), step)]

    def boundary(n, c, to):
        i = first_of[n] + c
        return remote(piece(n, pairs[n][0], c), piece(n, pairs[n][1], c), first_sem.at[i], from_z.at[i], to)

    def onward(n, c, to):
        i = first_of[n] + c
        return remote(piece(n, pairs[n][1], c), piece(n, pairs[n][1], c), fwd_sem.at[i], from_z.at[i], to)

    def sideways(n, c):
        i = first_of[n] + c
        return remote(piece(n, pairs[n][1], c), piece(n, pairs[n][1], c), side_sem.at[i], from_y.at[i], sibling)

    def each(body):
        for n in range(3):
            def step(c, carry, n=n):
                body(n, c)
                return carry
            lax.fori_loop(0, pairs[n][2], step, 0)

    edge = jnp.logical_and(far, jnp.logical_or(p.zl == 0, p.zl == 15))
    outward = p.zglobal(jnp.where(p.zl == 0, -1, 1))
    inward = p.at(zl=p.zl + jnp.where(p.zl < 8, 1, -1))
    passes = jnp.logical_and(far, jnp.logical_and(p.zl != 7, p.zl != 8))

    @pl.when(edge)
    def _():
        each(lambda n, c: boundary(n, c, outward).start())

    own = pltpu.make_async_copy(send.at[p.me], recv.at[p.me], own_sem)
    own.start()

    def rows_to(k):
        h = lax.rem(p.me + k, 16)
        return remote(send.at[h], recv.at[p.me], send_sem.at[k], recv_sem.at[k], p.member(h))

    def every(first, body):
        def step(k, carry):
            body(k)
            return carry
        lax.fori_loop(first, 16, step, 0)

    @pl.when(jnp.logical_not(far))
    def _():
        every(1, lambda k: rows_to(k).start())
        kept = [pltpu.make_async_copy(pairs[n][0], pairs[n][1], keep_sem.at[n]) for n in range(3)]
        for copy in kept:
            copy.start()
        for copy in kept:
            copy.wait()

    @pl.when(far)
    def _():
        def take(n, c):
            onward(n, c, inward).wait_recv()

            @pl.when(passes)
            def _():
                onward(n, c, inward).start()

            sideways(n, c).start()

            @pl.when(first_of[n] + c < 15)
            def _():
                rows_to(first_of[n] + c + 1).start()

        each(take)
        each(lambda n, c: sideways(n, c).wait())

    @pl.when(passes)
    def _():
        each(lambda n, c: onward(n, c, inward).wait_send())

    @pl.when(edge)
    def _():
        each(lambda n, c: boundary(n, c, outward).wait_send())

    own.wait()
    every(1, lambda k: rows_to(k).wait())


def dispatch(send, gate, up, down):
    dma = pltpu.SemaphoreType.DMA
    return pl.pallas_call(
        dispatch_kernel,
        out_shape=[jax.ShapeDtypeStruct(v.shape, v.dtype) for v in (send, gate, up, down)],
        in_specs=[ANY] * 4,
        out_specs=[ANY] * 4,
        scratch_shapes=[
            dma((16,)), dma((16,)), dma(()), dma((22,)), dma((22,)), dma((22,)), dma((22,)), dma((22,)), dma((3,)),
        ],
        compiler_params=pltpu.CompilerParams(collective_id=0, has_side_effects=True, vmem_limit_bytes=LIMIT),
    )(send, gate, up, down)


def expert_kernel(recv, gate, up, down, back, part):
    f32, bf16 = jnp.float32, jnp.bfloat16
    sources, both, width = recv.shape
    capacity, units = both // 2, gate.shape[1]
    wide = recv[...].astype(f32)
    arrived = wide[:, :capacity].reshape(-1, width).astype(bf16)
    d_arrived = wide[:, capacity:].reshape(-1, width).astype(bf16)
    pre_gate = jnp.dot(arrived, gate[...], preferred_element_type=f32)
    pre_up = jnp.dot(arrived, up[...], preferred_element_type=f32)
    d_hidden = lax.dot_general(d_arrived, down[...], contract_cols, preferred_element_type=f32)
    sigmoid_gate = jax.nn.sigmoid(pre_gate)
    active = pre_gate * sigmoid_gate
    hidden = (active * pre_up).astype(bf16)
    d_pre_gate = (d_hidden * pre_up * sigmoid_gate * (1.0 + pre_gate * (1.0 - sigmoid_gate))).astype(bf16)
    d_pre_up = (d_hidden * active).astype(bf16)
    produced = jnp.dot(hidden, down[...], preferred_element_type=f32)
    d_back = lax.dot_general(
        d_pre_gate, gate[...], contract_cols, preferred_element_type=f32
    ) + lax.dot_general(d_pre_up, up[...], contract_cols, preferred_element_type=f32)
    back[...] = jnp.concatenate(
        [produced.reshape(sources, capacity, width), d_back.reshape(sources, capacity, width)], axis=1
    ).astype(bf16)
    for n, (left, right) in enumerate(((arrived, d_pre_gate), (arrived, d_pre_up), (d_arrived, hidden))):
        part[:, n * units : (n + 1) * units] = lax.dot_general(
            left, right, contract_rows, preferred_element_type=f32
        ).astype(bf16)


def expert(recv, gate, up, down):
    return pl.pallas_call(
        expert_kernel,
        out_shape=[
            jax.ShapeDtypeStruct(recv.shape, recv.dtype),
            jax.ShapeDtypeStruct((recv.shape[2], 3 * gate.shape[1]), jnp.bfloat16),
        ],
        in_specs=[VMEM] * 4,
        out_specs=[VMEM] * 2,
        compiler_params=pltpu.CompilerParams(vmem_limit_bytes=LIMIT),
    )(recv, gate, up, down)


def finish_kernel(
    send, part, pull, tokens, normed, grad, columns, signs, router, gain,
    layer_out, d_tokens, share, small_out,
    recv, y_got, held, z_got, total, got, exact, leaving, native, other, small, g1, g2, g3, g4, whole,
    send_sem, recv_sem, own_sem, y_send, y_recv, z_send, z_recv, w_send, w_recv, f_send, f_recv,
    s1, r1, s2, r2, s3, r3, s4, r4, s5, r5,
):
    f32, bf16 = jnp.float32, jnp.bfloat16
    p = Place()
    xc = p.x * 2 + p.core
    ci = p.zh * 4 + p.a

    def xc_at(t):
        return p.at(x=lax.div(t, 2), core=lax.rem(t, 2))

    def y_at(t):
        return p.at(y=t)

    def b_at(t):
        return p.at(zl=p.a * 4 + t)

    def c_at(t):
        return p.at(zl=lax.rem(t, 4) * 4 + p.b, zh=lax.div(t, 4))

    near = p.far == 0
    for k in range(1, 16):
        signal(p.member(lax.rem(p.me + k, 16)))
    for k in range(1, 8):
        signal(c_at(lax.rem(ci + k, 8)))
    for k in range(1, 4):
        signal(y_at(lax.rem(p.y + k, 4)))
        signal(b_at(lax.rem(p.b + k, 4)))
    pair = 2 * p.side + lax.rem(p.y + 1, 2)
    signal(p.at(y=pair, zh=1 - p.zh))
    pl.semaphore_wait(pltpu.get_barrier_semaphore(), 29)

    y_copies = []
    for k in range(4):
        bb = lax.rem(p.b + k + 1, 4)
        copy = remote(part.at[:, bb, 1 - p.side], y_got.at[:, bb], y_send.at[k], y_recv.at[k], p.at(y=3 - p.y))
        copy.start()
        y_copies.append(copy)
    own, copies = exchange(p, send, recv, send_sem, recv_sem, own_sem)
    z_copies = []
    for k in range(4):
        bb = lax.rem(p.b + k + 1, 4)
        y_copies[k].wait_recv()
        held[k] = (part[:, bb, p.side].astype(f32) + y_got[:, bb].astype(f32)).astype(bf16)
        if k < 3:
            copy = remote(held.at[k], z_got.at[k], z_send.at[k], z_recv.at[k], b_at(bb))
            copy.start()
            z_copies.append(copy)

    for copy in z_copies:
        copy.wait()
    summed = held[3].astype(f32)
    for k in range(3):
        summed = summed + z_got[k].astype(f32)
    total[...] = summed.astype(bf16).reshape(total.shape)

    w_copies = []
    for k in range(1, 4):
        aa = lax.rem(p.a + k, 4)
        copy = remote(total.at[aa], got.at[k - 1], w_send.at[k], w_recv.at[k], p.at(zl=aa * 4 + p.b))
        copy.start()
        w_copies.append(copy)

    own.wait()
    for copy in copies:
        copy.wait()
    returned = recv[...].reshape(-1, recv.shape[2])
    tok = tokens.shape[0]
    inverse, gate_0, gate_1 = columns[:, 0:1], columns[:, 1:2], columns[:, 2:3]
    rows_0 = jnp.dot(pull[:tok], returned, preferred_element_type=f32)
    rows_1 = jnp.dot(pull[tok : 2 * tok], returned, preferred_element_type=f32)
    layer_out[...] = (gate_0 * rows_0 + gate_1 * rows_1).astype(bf16)
    upstream = grad[...].astype(f32)
    d_pair_0 = jnp.sum(upstream * rows_0, axis=1, keepdims=True)
    d_pair_1 = jnp.sum(upstream * rows_1, axis=1, keepdims=True)
    d_logits = signs[...] * (gate_0 * gate_1 * (d_pair_0 - d_pair_1))
    high = d_logits.astype(bf16)
    rest = d_logits - high.astype(f32)
    middle = rest.astype(bf16)
    low = (rest - middle.astype(f32)).astype(bf16)
    d_normed = jnp.dot(pull[2 * tok :], returned, preferred_element_type=f32)
    for term in (low, middle, high):
        d_normed = d_normed + jnp.dot(term, router[...], preferred_element_type=f32)
    router_term = jnp.zeros((signs.shape[1], normed.shape[1]), f32)
    for term in (low, middle, high):
        router_term = router_term + lax.dot_general(term, normed[...], contract_rows, preferred_element_type=f32)
    experts = signs.shape[1]
    unit_rows = tokens[...].astype(f32) * inverse
    product = d_normed * unit_rows
    small[:experts] = router_term
    small[experts:] = jnp.broadcast_to(jnp.sum(product, axis=0, keepdims=True), (8, normed.shape[1]))
    scaled = d_normed * gain[...]
    mean = jnp.sum(product * gain[...], axis=1, keepdims=True) * (1.0 / normed.shape[1])
    d_tokens[...] = (inverse * (scaled - unit_rows * mean)).astype(bf16)

    def lanes(t):
        return pl.ds(pl.multiple_of(t * 128, 128), 128)

    first = []
    for k in range(1, 8):
        t = lax.rem(xc + k, 8)
        copy = remote(small.at[:, lanes(t)], g1.at[k], s1.at[k], r1.at[k], xc_at(t))
        copy.start()
        first.append(copy)

    value = small[:, lanes(xc)]
    for copy in first:
        copy.wait()
    for k in range(1, 8):
        value = value + g1[k]

    def everywhere(value, slots, n, index, where, send_sem, recv_sem):
        slots[index] = value
        copies = []
        for k in range(1, n):
            copy = remote(
                slots.at[index], slots.at[index], send_sem.at[k], recv_sem.at[k], where(lax.rem(index + k, n))
            )
            copy.start()
            copies.append(copy)
        for copy in copies:
            copy.wait()
        value = slots[0]
        for k in range(1, n):
            value = value + slots[k]
        return value

    value = everywhere(value, g2, 4, p.y, y_at, s2, r2)
    value = everywhere(value, g3, 4, p.b, b_at, s3, r3)

    for copy in w_copies:
        copy.wait()
    block = total[p.a].astype(f32)
    for k in range(3):
        block = block + got[k].astype(f32)
    exact[...] = block
    leaving[...] = block.astype(bf16)
    here, there = lax.rem(p.y, 2), lax.rem(p.y + 1, 2)
    to_pair = remote(leaving.at[there], native, f_send.at[0], f_recv.at[0], p.at(y=pair))
    over_same = remote(leaving.at[here], other, f_send.at[0], f_recv.at[1], p.at(zh=1 - p.zh))
    over_pair = remote(leaving.at[there], other, f_send.at[1], f_recv.at[1], p.at(y=pair, zh=1 - p.zh))

    @pl.when(near)
    def _():
        to_pair.start()

    @pl.when(jnp.logical_not(near))
    def _():
        over_same.start()
        over_pair.start()

    value = everywhere(value, g4, 8, ci, c_at, s4, r4)
    whole[...] = value
    small_out[:, lanes(xc)] = value
    last = []
    for k in range(1, 8):
        copy = remote(whole, small_out.at[:, lanes(xc)], s5.at[k], r5.at[k], xc_at(lax.rem(xc + k, 8)))
        copy.start()
        last.append(copy)

    over_same.wait_recv()

    @pl.when(near)
    def _():
        to_pair.wait_send()
        share[...] = exact[here] + other[...].astype(f32)

    @pl.when(jnp.logical_not(near))
    def _():
        over_same.wait_send()
        over_pair.wait_send()
        to_pair.wait_recv()
        share[...] = native[...].astype(f32) + other[...].astype(f32)

    for copy in y_copies:
        copy.wait_send()
    for copy in last:
        copy.wait()


def finish(send, part, pull, tokens, normed, grad, columns, signs, router, gain):
    dma = pltpu.SemaphoreType.DMA
    rows, width = part.shape[3] // 2, part.shape[4]
    features, tall = tokens.shape[1], signs.shape[1] + 8
    f32, bf16 = jnp.float32, jnp.bfloat16
    block = (4, 2 * rows, width)
    return pl.pallas_call(
        finish_kernel,
        out_shape=[
            jax.ShapeDtypeStruct(tokens.shape, bf16),
            jax.ShapeDtypeStruct(tokens.shape, bf16),
            jax.ShapeDtypeStruct((rows, width), f32),
            jax.ShapeDtypeStruct((tall, features), f32),
        ],
        in_specs=[ANY] + [VMEM] * 9,
        out_specs=[VMEM] * 4,
        scratch_shapes=[
            pltpu.VMEM(send.shape, bf16),
            pltpu.VMEM((4,) + block, bf16),
            pltpu.VMEM((4,) + block, bf16),
            pltpu.VMEM((3,) + block, bf16),
            pltpu.VMEM((4, 2, rows, width), bf16),
            pltpu.VMEM((3, 2, rows, width), bf16),
            pltpu.VMEM((2, rows, width), f32),
            pltpu.VMEM((2, rows, width), bf16),
            pltpu.VMEM((rows, width), bf16),
            pltpu.VMEM((rows, width), bf16),
            pltpu.VMEM((tall, features), f32),
            pltpu.VMEM((8, tall, 128), f32),
            pltpu.VMEM((4, tall, 128), f32),
            pltpu.VMEM((4, tall, 128), f32),
            pltpu.VMEM((8, tall, 128), f32),
            pltpu.VMEM((tall, 128), f32),
            dma((16,)), dma((16,)), dma(()), dma((4,)), dma((4,)), dma((3,)), dma((3,)),
            dma((4,)), dma((4,)), dma((2,)), dma((2,)),
            dma((8,)), dma((8,)), dma((4,)), dma((4,)), dma((4,)), dma((4,)),
            dma((8,)), dma((8,)), dma((8,)), dma((8,)),
        ],
        compiler_params=pltpu.CompilerParams(collective_id=1, has_side_effects=True, vmem_limit_bytes=LIMIT),
    )(send, part, pull, tokens, normed, grad, columns, signs, router, gain)


def local(tokens, norm_gain, router_w, w_gate, w_up, w_down, routes, grad_out):
    f32, bf16 = jnp.float32, jnp.bfloat16
    tok_dev, width = tokens.shape
    experts = lax.axis_size("expert")
    capacity = max(2, 3 * tok_dev * TOP // (2 * experts))
    tokens_wide = tokens.astype(f32)
    inverse = lax.rsqrt(jnp.mean(tokens_wide * tokens_wide, axis=1, keepdims=True) + 1e-06)
    unit_rows = tokens_wide * inverse
    normed = (unit_rows * norm_gain).astype(bf16)
    logits = jnp.dot(normed, router_w, preferred_element_type=f32)
    expert_ids = jnp.arange(experts, dtype=jnp.int32)[None, :]
    chosen = [routes[:, k : k + 1] == expert_ids for k in range(TOP)]
    picked = [jnp.sum(jnp.where(hot, logits, 0.0), axis=1) for hot in chosen]
    gate_pair = [jax.nn.sigmoid(picked[0] - picked[1]), jax.nn.sigmoid(picked[1] - picked[0])]

    token_ids = jnp.arange(tok_dev, dtype=jnp.int32)
    earlier = (token_ids[:, None] > token_ids[None, :]).astype(bf16)
    named = jnp.logical_or(chosen[0], chosen[1]).astype(bf16)
    ahead = jnp.dot(earlier, named, preferred_element_type=f32)
    slots = [
        routes[:, k] * (2 * capacity) + jnp.sum(jnp.where(chosen[k], ahead, 0.0), axis=1).astype(jnp.int32)
        for k in range(TOP)
    ]
    places = jnp.arange(experts * 2 * capacity, dtype=jnp.int32)
    hits = [places[:, None] == slot[None, :] for slot in slots]
    d_hits = [places[:, None] == slot[None, :] + capacity for slot in slots]
    pick = jnp.concatenate(
        [jnp.logical_or(hits[0], hits[1]).astype(bf16), jnp.logical_or(d_hits[0], d_hits[1]).astype(bf16)], axis=1
    )
    scale = jnp.sum(
        jnp.where(d_hits[0], gate_pair[0][None, :], 0.0) + jnp.where(d_hits[1], gate_pair[1][None, :], 0.0), axis=1
    )
    is_row = lax.rem(places, 2 * capacity) < capacity
    scale = jnp.where(is_row, 1.0, scale)
    stacked = jnp.concatenate([normed, grad_out], axis=0)
    send = (jnp.dot(pick, stacked, preferred_element_type=f32) * scale[:, None]).astype(bf16)
    arrived_both, gate_local, up_local, down_local = dispatch(
        send.reshape(experts, 2 * capacity, width), w_gate[0], w_up[0], w_down[0]
    )
    back, joined = expert(arrived_both, gate_local, up_local, down_local)
    part = joined.reshape(4, 4, 2, 2 * (width // lax.axis_size("dp")), joined.shape[1])
    hidden_units = w_gate.shape[2]
    pull = jnp.concatenate(
        [
            slots[0][:, None] == places[None, :],
            slots[1][:, None] == places[None, :],
            jnp.logical_or(
                slots[0][:, None] + capacity == places[None, :], slots[1][:, None] + capacity == places[None, :]
            ),
        ],
        axis=0,
    ).astype(bf16)
    columns = jnp.concatenate([inverse, gate_pair[0][:, None], gate_pair[1][:, None]], axis=1)
    signs = chosen[0].astype(f32) - chosen[1].astype(f32)
    layer_out, d_tokens, share, small = finish(
        back, part, pull, tokens, normed, grad_out, columns, signs, jnp.transpose(router_w), norm_gain[None, :]
    )
    return (
        layer_out,
        d_tokens,
        small[experts],
        jnp.transpose(small[:experts]),
        share[None, :, :hidden_units],
        share[None, :, hidden_units : 2 * hidden_units],
        jnp.transpose(share[:, 2 * hidden_units :])[None],
    )


def solution(mesh):
    rows, experts, copied = P(("dp", "expert"), None), P("expert", None, None), P()
    return jax.shard_map(
        local,
        mesh=mesh,
        in_specs=(rows, copied, copied, experts, experts, experts, rows, rows),
        out_specs=(
            rows,
            rows,
            copied,
            copied,
            P("expert", "dp", None),
            P("expert", "dp", None),
            P("expert", None, "dp"),
        ),
        check_vma=False,
    )
```

time: 215 us -> 205 us (0.953)
  the two profiles are of different devices: /device:TPU:25 before, /device:TPU:101 now
where the time goes in v2:
time: 205 us; the launch traced here: 204 us
  Pallas kernels  188 us (92%)
  local copies, waits for them, and re-layouts  7.24 us (4%)
  matrix products  4 us (2%)
  other arithmetic  3.82 us (2%)
    pallas_call x1, Pallas kernels, finish(): pl.pallas_call(finish_kernel, out_shape=[jax.ShapeDtypeStruct(tokens.shap...  124 us
    pallas_call x1, Pallas kernels, dispatch(): pl.pallas_call(dispatch_kernel, out_shape=[jax.ShapeDtypeStruct(v.shape,...  58.6 us
    pallas_call x1, Pallas kernels, expert(): pl.pallas_call(expert_kernel, out_shape=[jax.ShapeDtypeStruct(recv.shape,...  5.51 us
    unnamed x22, local copies, waits for them, and re-layouts  4.51 us

profile of v2, /device:TPU:101, one launch (start us, length us, event | category | flops | bytes accessed | tf_op | source)
XLA Modules:
  0.0 204.2 jit_solution(9660273135146710272)
XLA Ops:
  0.6 0.8 slice_bitcast_fusion.4
  1.4 0.2 fusion.13
  1.6 0.0 copy-start.3
  1.6 0.0 copy-start.4
  1.6 0.0 copy-start.5
  1.6 1.2 fusion.3
  2.9 1.1 fusion.5.normed
  4.0 1.1 select_reduce_fusion.1
  5.1 0.8 broadcast_add_fusion.1
  5.8 0.1 fusion.9
  6.0 0.2 add_reduce_fusion
  6.2 2.7 %multiply_convert_fusion = bf16[768,1024]{1,0:T(8,128)(2,1)} fusion(f32[768]{0:T(1024)S(1)} %fusion.17, pred[768,128]{1,0:T(32,128)(4,1)S(1)} %get-tuple-element.55, pred[768,128]{1,0:T(32,128)(4,1)S(1)} %get-tuple-element.56, bf16[128,1024]{1,0:T(8,128)(2,1)} %grad.1, bf16[128,1024]{1,0:T(8,128)(2,1)S(1)} %fusion.5.normed), kind=kOutput, calls=%fused_computation | convolution fusion | flops 405471232 | bytes 2296832 | tf_op jit(solution)/shard_map/dot_general | solution.py:501
  8.9 0.0 copy-done.3
  8.9 0.0 copy-done.4
  8.9 0.0 copy-done.5
  8.9 58.6 %shard_map.135 = (bf16[16,48,1024]{2,1,0:T(8,128)(2,1)}, bf16[1024,384]{1,0:T(8,128)(2,1)S(1)}, bf16[1024,384]{1,0:T(8,128)(2,1)S(1)}, bf16[384,1024]{1,0:T(8,128)(2,1)S(1)}) custom-call(bf16[16,48,1024]{2,1,0:T(8,128)(2,1)} %bitcast.60, bf16[1024,384]{1,0:T(8,128)(2,1)S(1)} %bitcast.55, bf16[1024,384]{1,0:T(8,128)(2,1)S(1)} %bitcast.56, ...), custom_call_target="tpu_custom_call" | custom-call | tf_op jit(solution)/shard_map/pallas_call | solution.py:187
  67.5 0.0 copy-start.9
  67.6 0.0 copy-start.2
  67.6 1.4 copy-done.2
  69.0 0.0 copy-start
  69.0 0.0 copy-start.6
  69.0 0.0 copy-start.7
  69.0 0.0 copy-start.8
  69.0 5.5 %shard_map.136 = (bf16[16,48,1024]{2,1,0:T(8,128)(2,1)S(1)}, bf16[1024,1152]{1,0:T(8,128)(2,1)}) custom-call(bf16[16,48,1024]{2,1,0:T(8,128)(2,1)S(1)} %copy-done.2, bf16[1024,384]{1,0:T(8,128)(2,1)S(1)} %get-tuple-element.18.gate, bf16[1024,384]{1,0:T(8,128)(2,1)S(1)} %get-tuple-element.19.up, bf16[384,1024]{1,0:T(8,128)(2,1)S(1)} %get-tuple-element.20.down), custom_call_target="tpu_custom_call" | custom-call | tf_op jit(solution)/shard_map/pallas_call | solution.py:228
  74.5 0.0 copy-done.9
  74.5 0.2 iota_compare_fusion.2
  74.7 0.1 fusion.11
  74.9 0.1 copy.31.columns
  75.0 0.0 copy-done
  75.0 0.0 copy-done.6
  75.0 0.0 copy-done.7
  75.0 0.0 copy-done.8
  75.0 0.0 copy-start.1
  75.1 1.7 copy-done.1
  76.7 124.2 %shard_map.137 = (bf16[128,1024]{1,0:T(8,128)(2,1)S(1)}, bf16[128,1024]{1,0:T(8,128)(2,1)S(1)}, f32[16,1152]{1,0:T(8,128)S(1)}, f32[24,1024]{1,0:T(8,128)S(1)}) custom-call(bf16[16,48,1024]{2,1,0:T(8,128)(2,1)S(1)} %get-tuple-element.21.send, bf16[4,4,2,32,1152]{4,3,2,1,0:T(8,128)(2,1)S(1)} %bitcast.54, bf16[384,768]{1,0:T(8,128)(2,1)S(1)} %add_convert_fusion.pull, ...), custom_call_target="tpu_custom_call" | custom-call | tf_op jit(solution)/shard_map/pallas_call | solution.py:430
  200.9 0.6 slice_bitcast_fusion.1
  201.6 0.6 slice_bitcast_fusion
  202.2 0.6 slice.25
  202.8 0.7 copy.40
  203.5 0.7 copy.41
  (6 shorter events, 0.1 us)
Async XLA Ops:
  1.6 7.3 %copy-start.3 = (bf16[1,1024,384]{2,1,0:T(8,128)(2,1)S(1)}, bf16[1,1024,384]{2,1,0:T(8,128)(2,1)}, u32[]{:S(2)}) copy-start(bf16[1,1024,384]{2,1,0:T(8,128)(2,1)} %param.11) | copy-start | bytes 2359300
  1.6 7.3 %copy-start.4 = (bf16[1,1024,384]{2,1,0:T(8,128)(2,1)S(1)}, bf16[1,1024,384]{2,1,0:T(8,128)(2,1)}, u32[]{:S(2)}) copy-start(bf16[1,1024,384]{2,1,0:T(8,128)(2,1)} %param.12) | copy-start | bytes 2359300
  1.6 7.3 %copy-start.5 = (bf16[1,384,1024]{2,1,0:T(8,128)(2,1)S(1)}, bf16[1,384,1024]{2,1,0:T(8,128)(2,1)}, u32[]{:S(2)}) copy-start(bf16[1,384,1024]{2,1,0:T(8,128)(2,1)} %param.13) | copy-start | bytes 2359300
  67.5 7.0 %copy-start.9 = (s32[128,2]{0,1:T(2,128)S(1)}, s32[128,2]{0,1:T(2,128)}, u32[]{:S(2)}) copy-start(s32[128,2]{0,1:T(2,128)} %param.14) | copy-start | bytes 3076
  67.6 1.4 copy-start.2
  69.0 6.0 %copy-start = (bf16[128,1024]{1,0:T(8,128)(2,1)S(1)}, bf16[128,1024]{1,0:T(8,128)(2,1)}, u32[]{:S(2)}) copy-start(bf16[128,1024]{1,0:T(8,128)(2,1)} %tokens.1) | copy-start | bytes 786436
  69.0 6.1 %copy-start.6 = (bf16[128,1024]{1,0:T(8,128)(2,1)S(1)}, bf16[128,1024]{1,0:T(8,128)(2,1)}, u32[]{:S(2)}) copy-start(bf16[128,1024]{1,0:T(8,128)(2,1)} %grad.1) | copy-start | bytes 786436
  69.0 6.1 %copy-start.7 = (bf16[1024,16]{0,1:T(8,128)(2,1)S(1)}, bf16[1024,16]{0,1:T(8,128)(2,1)}, u32[]{:S(2)}) copy-start(bf16[1024,16]{0,1:T(8,128)(2,1)} %param.10) | copy-start | bytes 98308
  69.0 6.1 %copy-start.8 = (f32[1024]{0:T(1024)S(1)}, f32[1024]{0:T(1024)}, u32[]{:S(2)}) copy-start(f32[1024]{0:T(1024)} %param.9) | copy-start | bytes 12292
  75.0 1.7 copy-start.1
